TPU v7x, 256 devices: a whole 4x4x8 slice. The times are simulated.
256 devices in a mesh: samp: 8 (over x, z_lo), par: 32 (over y, z_hi, core).
Axes of the slice: x: 4, y: 4, z: 8 (z_hi: 4, z_lo: 2; z = z_hi * 2 + z_lo), core: 2. Of those that a mesh axis runs over, the one named last changes fastest.
Arguments:
- log_derivs: float32 [4096, 32768], P('samp', 'par')
- spins: int32 [4096, 100], P('samp'), may hold values from 0 to 1
- roster: int32 [2, 512], replicated, may hold values from 0 to 4095, as said below
Outputs:
- gram_tiles: float32 [8, 3, 512, 512], P('samp', None, 'par')
Inputs may be any that keep to these rules, and one draw needn't show every extreme that they name: In each round r all entries share one quotient m_r = roster[r, j] // 512; the m_r of different rounds are distinct and one of them is 7; the remainders roster[r, j] % 512 of a round are a permutation of 0 to 511.
All inputs are finite; a program needn't handle non-finite values.
Results may differ from a plain program's by a relative error of at most 0.0003.
Values sent between devices are 32-bit elements; how exact they have to be, the bound alone decides.
A program may use at most 64 MiB of HBM per device.

v0:
```python
import functools

import jax
import jax.numpy as jnp
from jax import lax
from jax.experimental import pallas as pl
from jax.experimental.pallas import tpu as pltpu
from jax.sharding import PartitionSpec as P

MESH = pl.DeviceIdType.MESH
F32, BF16 = jnp.float32, jnp.bfloat16

SG = 512
NSITES = 100
LSIDE = 10
COLS = 1024
HALF = COLS // 2
SAMPLES = 4096
SUBS = 32
LAG = 7
SLOTS = SUBS + LAG
SENDS = 24
LAST = 5
CHUNKS = 4


def bit_of(value, index):
    return lax.rem(lax.div(value, jnp.int32(2**index)), jnp.int32(2))


def flip(value, mask, bits):
    total = jnp.int32(0)
    for index in range(bits):
        bit = bit_of(value, index)
        total = total + (1 - bit if mask >> index & 1 else bit) * 2**index
    return total


def dot_nt(left, right):
    return lax.dot_general(left, right, (((1,), (1,)), ((), ())), preferred_element_type=F32)


def split(value):
    high = value.astype(BF16)
    return high, (value - high.astype(F32)).astype(BF16)


def product(left, right):
    (left_high, left_low), (right_high, right_low) = left, right
    return dot_nt(left_high, right_high) + (dot_nt(left_high, right_low) + dot_nt(left_low, right_high))


def kernel(x_hbm, spins_hbm, roster_hbm, out_ref, *scratch):
    (rows, spins_ref, roster_ref, own, stage_x, stage_z, stage_1, got_x, got_z, got_1, sums, mean_ref,
     c_high, c_low, h_high, h_low, b_high, b_low, pay_d, pay_a, pay_b, r0_d, r0_c, r1_d, r1_c,
     r2_d, r2_c, r3_d, r3_c, r4_d, r4_c, cross_7, cross_m, picks,
     load_sem, send_sem, recv_sem) = scratch
    group = lax.axis_index("samp")
    part = lax.axis_index("par")
    core = lax.rem(part, jnp.int32(2))
    zh = lax.rem(lax.div(part, jnp.int32(2)), jnp.int32(4))
    y = lax.div(part, jnp.int32(8))

    def samp_peer(mask):
        return {"samp": flip(group, mask, 3)}

    def par_peer(new_y, new_zh, new_core):
        return {"par": new_y * 8 + new_zh * 2 + new_core}

    sibling = par_peer(y, zh, 1 - core)
    load_spins = pltpu.make_async_copy(spins_hbm, spins_ref, load_sem.at[4])
    load_roster = pltpu.make_async_copy(roster_hbm, roster_ref, load_sem.at[5])
    loads = [
        pltpu.make_async_copy(x_hbm.at[:, :, k % 2, k // 2], rows.at[k], load_sem.at[k]) for k in range(CHUNKS)
    ]
    for load in (load_roster, load_spins, *loads):
        load.start()

    peers = [samp_peer(mask) for mask in range(7, 0, -1)]
    peers += [par_peer(y, flip(zh, mask, 2), core) for mask in (1, 3)]
    peers += [par_peer(flip(y, mask, 2), zh, core) for mask in (1, 3)]
    peers += [sibling]
    barrier = pltpu.get_barrier_semaphore()
    for peer in peers:
        pl.semaphore_signal(barrier, inc=1, device_id=peer, device_id_type=MESH)

    def scope(name):
        return jax.named_scope(name)

    counter = [0]
    turn_of_send = [0]
    open_sends = [[] for _ in range(SENDS)]

    def fresh():
        counter[0] += 1
        return counter[0] - 1

    def remote(src, dst, peer, index, send_index):
        return pltpu.make_async_remote_copy(
            src_ref=src, dst_ref=dst, send_sem=send_sem.at[send_index], recv_sem=recv_sem.at[index],
            device_id=peer, device_id_type=MESH,
        )

    def wait_sends(slot):
        for gate, copy in open_sends[slot]:
            if gate is None:
                copy.wait_send()
            else:
                pl.when(gate)(copy.wait_send)
        open_sends[slot] = []

    def start(choices, peer, index):
        slot = turn_of_send[0] % SENDS
        turn_of_send[0] += 1
        wait_sends(slot)
        copies = []
        for gate, src, dst in choices:
            copy = remote(src, dst, peer, index, slot)
            if gate is None:
                copy.start()
            else:
                pl.when(gate)(copy.start)
            copies.append((gate, copy))
        open_sends[slot] = copies
        return copies

    load_roster.wait()
    masks = lax.shift_right_logical(roster_ref[...], 9)
    within = roster_ref[...] & (SG - 1)
    seven_first = masks[0:1] == 7
    other = jnp.where(seven_first, masks[1:2], masks[0:1])
    bits = [bit_of(group, index) for index in range(3)]
    side = jnp.where(other == 4, bits[2], jnp.where((other == 2) | (other == 6), bits[1], bits[0]))
    m_part = jnp.broadcast_to(other, (16, SG))
    z_first = (m_part == 1) | (m_part == 3)

    load_spins.wait()
    site = lax.broadcasted_iota(jnp.int32, (NSITES, SG), 0)
    on_a = lax.rem(lax.div(site, jnp.int32(LSIDE)) + lax.rem(site, jnp.int32(LSIDE)), jnp.int32(2)) == 0
    count = jnp.sum(jnp.where(on_a, spins_ref[...], 0).astype(F32), axis=0, keepdims=True)
    sign_row = 1.0 - 2.0 * (count - 2.0 * jnp.floor(count * 0.5))
    sign = jnp.transpose(jnp.broadcast_to(sign_row, (128, SG)))[:, 0:1].reshape(4, 4, 2, 2, 8, 1)
    side128 = jnp.broadcast_to(side, (128, SG)) == 1
    hops = {"x": [], "z": [], "1": []}
    hop_masks = {"x": 6, "z": 1, "1": 2}
    hop_sems = {hop: [fresh() for _ in range(2 * (LAST if hop == "1" else LAG))] for hop in hops}
    hop_sends = {hop: [SENDS + index for index in sems] for hop, sems in hop_sems.items()}

    def send_hop(hop, src, dst):
        sems, copies = hop_sems[hop], hops[hop]
        if len(copies) >= len(sems):
            copies[-len(sems)].wait_send()
        turn = len(copies) % len(sems)
        copy = remote(src, dst, samp_peer(hop_masks[hop]), sems[turn], hop_sends[hop][turn])
        copy.start()
        copies.append(copy)

    def exchange(slot):
        before = slot - LAG
        if 0 <= before < SLOTS:
            for hop in "xz":
                hops[hop][before].wait_recv()
        if slot < SLOTS:
            if slot < LAG:
                from_x = from_z = own.at[slot]
            elif slot < SUBS:
                stage_x[slot] = jnp.where(z_first, got_z[before], own[slot])
                stage_z[slot] = jnp.where(z_first, own[slot], got_x[before])
                from_x, from_z = stage_x.at[slot], stage_z.at[slot]
            else:
                from_x, from_z = got_z.at[before], got_x.at[before]
            send_hop("x", from_x, got_x.at[slot])
            send_hop("z", from_z, got_z.at[slot])
        sub = slot - 2 * LAG - LAST
        for sub in range(sub, sub + 1) if slot < SUBS + 2 * LAG else range(sub, SUBS):
            if sub >= 0:
                hops["1"][sub].wait_recv()
        sub = slot - 2 * LAG
        if 0 <= sub < SUBS:
            stage_1[sub] = jnp.where(
                m_part == 2, own[sub],
                jnp.where(m_part == 3, got_z[sub], jnp.where(m_part == 4, got_x[sub], got_z[sub + LAG])),
            )
            send_hop("1", stage_1.at[sub], got_1.at[sub])

    column_sum = jnp.zeros((8, COLS), F32)
    for k in range(CHUNKS):
        loads[k].wait()
        signed = rows[k] * sign[:, :, k % 2, k // 2]
        rows[k] = signed
        column_sum = column_sum + jnp.sum(signed.reshape(16, 8, COLS), axis=0)
        flat = signed.reshape(128, COLS)
        own[pl.ds(8 * k, 8)] = jnp.where(side128, flat[:, :HALF], flat[:, HALF:]).reshape(8, 16, HALF)
    sums[0] = jnp.sum(column_sum, axis=0, keepdims=True)
    with scope("bar"):
        pl.semaphore_wait(barrier, len(peers))
    sum_copies = []
    for mask in range(1, 8):
        sum_copies += start([(None, sums.at[0], sums.at[mask])], samp_peer(mask), fresh())

    natural = lax.broadcasted_iota(jnp.int32, (1, SG), 1)
    plans = [
        natural,
        jnp.where(seven_first, within[0:1], within[1:2]),
        jnp.where(seven_first, within[1:2], within[0:1]),
    ]

    def place_picks(index):
        plan = plans[index]
        p = plan >> 4
        place = ((plan >> 3) & 1) * 256 + (p & 1) * 128 + (p >> 3) * 32 + ((p >> 1) & 3) * 8 + (plan & 7)
        for first in range(0, SG, 128):
            position = lax.broadcasted_iota(jnp.int32, (128, SG), 0) + first
            picks[index, pl.ds(first, 128)] = jnp.where(position == place, 1.0, 0.0).astype(BF16)

    def centre():
        for _, copy in sum_copies:
            copy.wait_recv()
        mean = (
            ((sums[0] + sums[1]) + (sums[2] + sums[3])) + ((sums[4] + sums[5]) + (sums[6] + sums[7]))
        ) * (1.0 / SAMPLES)
        mean_ref[...] = jnp.where(side == 1, mean[:, HALF:], mean[:, :HALF])
        for k in range(CHUNKS):
            at = pl.ds(k * 128, 128)
            centred = rows[k].reshape(128, COLS) - mean
            c_high[at], c_low[at] = split(centred)
            h_high[at], h_low[at] = split(jnp.where(side128, centred[:, HALF:], centred[:, :HALF]))

    order_of = ((0, 3, 1, 2), (0, 1, 2, 3))
    hop_pairs = ((1, 3), (3, 1))

    def pair_of(index, q):
        low, high = bit_of(index, 0), bit_of(index, 1)
        return lax.rem(low + high, jnp.int32(2)) if q == 0 else high

    def place_in(index, q):
        return bit_of(index, 1 - q)

    def diagonal(c, half):
        rows_at, at = pl.ds(c * 256, 256), pl.ds(half * 256, 256)
        tile = product((c_high[rows_at], c_low[rows_at]), (c_high[at], c_low[at])).reshape(2, 4, 4, 8, 256)
        for i, to_y in enumerate(order_of[c]):
            for j, to_zh in enumerate(order_of[c]):
                pay_d[:, c, i, j, :, at] = tile[:, to_y, to_zh]

    def gather(k, kind):
        for j in range(8):
            sub = 8 * k + j
            if kind == 0:
                part_rows = jnp.where(z_first, got_x[sub + LAG], got_z[sub + LAG])
            else:
                part_rows = jnp.where(m_part == 1, got_z[sub], jnp.where(m_part == 6, got_x[sub], got_1[sub]))
            at = pl.ds(kind * 128 + 16 * j, 16)
            b_high[at], b_low[at] = split(part_rows - mean_ref[...])

    def tiles(k, kinds):
        at = pl.ds(kinds[0] * 128, len(kinds) * 128)
        tile = product((h_high[...], h_low[...]), (b_high[at], b_low[at]))
        own_tile = tile.reshape(2, 2, 4, 4, 8, len(kinds) * 128)
        back_tile = jnp.transpose(tile).reshape(len(kinds), 4, 4, 8, SG)
        for index, q in enumerate(kinds):
            lanes = slice(index * 128, index * 128 + 128)
            for i, to_y in enumerate(order_of[q]):
                for j, to_zh in enumerate(order_of[q]):
                    pay_b[k, q, i, j] = back_tile[index, to_y, to_zh]
                    for c in range(2):
                        pay_a[k, :, q, i, j, :, pl.ds(c * 128, 128)] = own_tile[c, :, to_y, to_zh, :, lanes]

    def halving(r0, r1, r2, r3, r4, wide, qs=(0, 1), ready=None):
        def hop(src, dst, peer):
            if wide is None:
                return start([(None, src, dst)], peer, fresh())
            first = pl.ds(0, 256)
            return start([(wide[0], src, dst), (wide[1], src.at[..., first], dst.at[..., first])], peer, fresh())

        def arrive(copies):
            for gate, copy in copies:
                if gate is None:
                    copy.wait_recv()
                else:
                    pl.when(gate)(copy.wait_recv)

        def add(dst, at, other):
            if wide is None:
                dst[at] = dst[at] + other[...]
                return
            first, rest = pl.ds(0, 256), pl.ds(256, SG)
            dst[at + (Ellipsis, first)] = dst[at + (Ellipsis, first)] + other[..., first]

            @pl.when(wide[0])
            def _():
                dst[at + (Ellipsis, rest)] = dst[at + (Ellipsis, rest)] + other[..., rest]

        steps = {}
        for q in qs:
            near = hop_pairs[q][0]
            peer = par_peer(flip(y, near, 2), zh, core)
            steps[q] = hop(r0.at[q, pl.ds(2 * (1 - pair_of(y, q)), 2)], r1.at[q], peer)
        yield
        nexts = {}
        for q in qs:
            far = hop_pairs[q][1]
            pair, place = pair_of(y, q), place_in(y, q)
            arrive(steps[q])
            add(r1, (q, 1 - place), r0.at[q, 2 * pair + 1 - place])
            nexts[q] = hop(r1.at[q, 1 - place], r2.at[q], par_peer(flip(y, far, 2), zh, core))
        for q in qs:
            pair, place = pair_of(y, q), place_in(y, q)
            add(r1, (q, place), r0.at[q, 2 * pair + place])
        yield
        steps = {}
        for q in qs:
            near = hop_pairs[q][0]
            arrive(nexts[q])
            add(r2, (q,), r1.at[q, place_in(y, q)])
            peer = par_peer(y, flip(zh, near, 2), core)
            steps[q] = hop(r2.at[q, pl.ds(2 * (1 - pair_of(zh, q)), 2)], r3.at[q], peer)
        yield
        nexts = {}
        for q in qs:
            far = hop_pairs[q][1]
            pair, place = pair_of(zh, q), place_in(zh, q)
            arrive(steps[q])
            add(r3, (q, 1 - place), r2.at[q, 2 * pair + 1 - place])
            nexts[q] = hop(r3.at[q, 1 - place], r4.at[q], par_peer(y, flip(zh, far, 2), core))
        for q in qs:
            pair, place = pair_of(zh, q), place_in(zh, q)
            add(r3, (q, place), r2.at[q, 2 * pair + place])
        yield
        for q in reversed(qs):
            arrive(nexts[q])
            add(r4, (q,), r3.at[q, place_in(zh, q)])
            if ready is not None:
                ready(q)

    def reduce_diagonal():
        ((_, step),) = start([(None, pay_d.at[1 - core], r0_d)], sibling, fresh())
        yield
        step.wait_recv()
        r0_d[...] = r0_d[...] + pay_d[core]
        yield from halving(r0_d, r1_d, r2_d, r3_d, r4_d, None)

    cross_sems = [[fresh() for _ in range(7)] for _ in range(2)]

    def reduce_chunk(k, kinds):
        c, to = k // 2, k % 2
        here, there = core == to, core != to
        first, rest = pl.ds(0, 256), pl.ds(256, SG)
        at = pl.ds(kinds[0], len(kinds))
        (_, step_a), (_, step_b) = start(
            [
                (here, pay_a.at[k, 1 - core, at], r0_c.at[k, at, ..., first]),
                (there, pay_b.at[k, at], r0_c.at[k, at, ..., rest]),
            ],
            sibling,
            fresh(),
        )
        yield

        @pl.when(there)
        def _():
            step_a.wait_recv()
            r0_c[k, at, ..., first] = r0_c[k, at, ..., first] + pay_a[k, 1 - to, at]

        @pl.when(here)
        def _():
            step_b.wait_recv()
            for q in kinds:
                places = [(order_of[q].index(to_y), order_of[q].index(to_zh)) for to_y in range(4) for to_zh in range(4)]
                for half in range(2):
                    lanes = pl.ds(256 + half * 256 + to * 128, 128)
                    block = jnp.concatenate([r0_c[k, q, i, j, :, lanes] for i, j in places], axis=0)
                    block = jnp.transpose(block).reshape(16, 8, 128)
                    lanes = pl.ds(half * 128, 128)
                    for place, (i, j) in enumerate(places):
                        r0_c[k, q, i, j, :, lanes] = pay_a[k, to, q, i, j, :, lanes] + block[place]
            r0_c[k, at, ..., rest] = r0_c[k, at, ..., rest] + pay_b[k, at]

        crossings = []

        def cross_over(kind):
            for mask in (7,) if kind == 0 else (5, 4, 3, 6, 2, 1):
                to_ref = cross_7.at[c] if kind == 0 else cross_m.at[c, mask - 1]
                ((_, copy),) = start(
                    [(here, r4_c.at[k, kind, :, rest], to_ref)], samp_peer(mask), cross_sems[c][mask - 1]
                )
                crossings.append(copy)

        yield from halving(
            r0_c.at[k], r1_c.at[k], r2_c.at[k], r3_c.at[k], r4_c.at[k], (here, there), kinds, cross_over
        )
        yield

        @pl.when(here)
        def _():
            for copy in crossings:
                copy.wait_recv()

    def ordered(value, index):
        value = value * (1.0 / SAMPLES)
        high, low = split(value)
        rest = value - high.astype(F32) - low.astype(F32)
        stacked = jnp.concatenate([high, low, rest.astype(BF16)], axis=0)
        moved = lax.dot_general(stacked, picks[index], (((1,), (0,)), ((), ())), preferred_element_type=F32)
        return moved[0:16] + (moved[16:32] + moved[32:48])

    def whole(kind):
        blocks = []
        for c in range(2):
            own_part = jnp.concatenate([r4_c[k, kind, :, pl.ds(c * 128, 128)] for k in range(CHUNKS)], axis=1)
            if kind == 0:
                arrived = cross_7[c]
            else:
                arrived = cross_m[c, 0]
                for mask in range(2, 7):
                    arrived = jnp.where(other == mask, cross_m[c, mask - 1], arrived)
            blocks.append(own_part + arrived)
        return jnp.concatenate(blocks, axis=0)

    walks = {}

    def advance(name):
        next(walks[name], None)

    def begin(name, walk):
        walks[name] = walk
        advance(name)

    def make_d(index):
        diagonal(index // 2, index % 2)
        if index == 3:
            begin("d", reduce_diagonal())

    both = (0, 1)

    def make(k, kinds):
        for kind in kinds:
            gather(k, kind)
        tiles(k, kinds)
        begin((k, kinds), reduce_chunk(k, kinds))

    c0, c1, c2, c3 = ((k, both) for k in range(4))
    after = {
        0: [(place_picks, 0)],
        1: [(place_picks, 1)],
        2: [(place_picks, 2)],
        7: [(centre,)],
        9: [(make_d, 0)],
        11: [(make_d, 1)],
        13: [(make_d, 2)],
        15: [(make_d, 3)],
        24: [(advance, "d")],
        26: [(make, 0, both)],
        31: [(advance, "d")],
        33: [(advance, c0)],
        34: [(make, 1, both)],
        40: [(advance, c0)],
        41: [(advance, c1)],
        42: [(make, 2, both), (advance, "d")],
        45: [(advance, c0), (advance, c2)],
        46: [(make, 3, both)],
    }
    for slot in range(SUBS + 2 * LAG + 1):
        with scope(f"ex{slot}"):
            exchange(slot)
        for job, *about in after.get(slot, []):
            with scope(f"job{slot}_{job.__name__}_{about}"):
                job(*about)
    def finish_d():
        tile_d = jnp.concatenate([r4_d[0], r4_d[1]], axis=0)
        out_ref[0, 0] = ordered(tile_d, 0)
        return tile_d
    for turn, name in enumerate((c1, c3, "d", c0, c2, c3, c1, "d", "tile", c2, c3, c0, c1, c2, c3, c1, c2, c3, c0, c1, c2, c3)):
        with scope(f"tail{turn}_{name}"):
            if name == "tile":
                tile_d = finish_d()
            else:
                advance(name)
    with scope("final"):
        tile_7 = ordered(whole(0), 1)
        tile_m = ordered(jnp.where(other == 0, tile_d, whole(1)), 2)
        out_ref[0, 1] = jnp.where(seven_first, tile_7, tile_m)
        out_ref[0, 2] = jnp.where(seven_first, tile_m, tile_7)
    with scope("drain"):
        for hop, copies in hops.items():
            for copy in copies[-len(hop_sems[hop]):]:
                copy.wait_send()
        for slot in range(SENDS):
            wait_sends(slot)


def gram(x, spins, roster):
    vmem = pltpu.VMEM

    def halves(lead, width):
        return [
            vmem(lead + (2, 4, 4, 8, width), F32),
            vmem(lead + (2, 2, 4, 8, width), F32),
            vmem(lead + (2, 4, 8, width), F32),
            vmem(lead + (2, 2, 8, width), F32),
            vmem(lead + (2, 8, width), F32),
        ]

    sets = [halves((), SG), halves((CHUNKS,), 256 + SG)]
    scratch = [
        vmem((CHUNKS, 4, 4, 8, COLS), F32),
        vmem((NSITES, SG), jnp.int32),
        vmem((2, SG), jnp.int32),
        vmem((SUBS, 16, HALF), F32),
        vmem((SLOTS, 16, HALF), F32),
        vmem((SLOTS, 16, HALF), F32),
        vmem((SUBS, 16, HALF), F32),
        vmem((SLOTS, 16, HALF), F32),
        vmem((SLOTS, 16, HALF), F32),
        vmem((SUBS, 16, HALF), F32),
        vmem((8, 1, COLS), F32),
        vmem((1, HALF), F32),
        vmem((SG, COLS), BF16),
        vmem((SG, COLS), BF16),
        vmem((SG, HALF), BF16),
        vmem((SG, HALF), BF16),
        vmem((256, HALF), BF16),
        vmem((256, HALF), BF16),
        vmem((2, 2, 4, 4, 8, SG), F32),
        vmem((CHUNKS, 2, 2, 4, 4, 8, 256), F32),
        vmem((CHUNKS, 2, 4, 4, 8, SG), F32),
        *[one[step] for step in range(5) for one in sets],
        vmem((2, 8, SG), F32),
        vmem((2, 6, 8, SG), F32),
        vmem((3, SG, SG), BF16),
        pltpu.SemaphoreType.DMA((6,)),
        pltpu.SemaphoreType.DMA((SENDS + 4 * LAG + 2 * LAST,)),
        pltpu.SemaphoreType.DMA((104,)),
    ]
    return pl.pallas_call(
        kernel,
        out_shape=jax.ShapeDtypeStruct((1, 3, 16, SG), F32),
        in_specs=[pl.BlockSpec(memory_space=pltpu.HBM)] * 3,
        out_specs=pl.BlockSpec(memory_space=pltpu.VMEM),
        scratch_shapes=scratch,
        compiler_params=pltpu.CompilerParams(
            collective_id=0, has_side_effects=True, vmem_limit_bytes=55040 * 1024
        ),
        name="gram",
    )(x, spins, roster)


def on_device(log_derivs, spins, roster):
    return gram(log_derivs.reshape(4, 4, 2, 2, 8, COLS), spins.T, roster)


def solution(mesh):
    in_specs = (P("samp", "par"), P("samp", None), P())
    out_specs = P("samp", None, "par", None)
    return jax.shard_map(
        on_device, mesh=mesh, in_specs=in_specs, out_specs=out_specs, check_vma=False
    )
```

profile of v0, /device:TPU:1, one launch (start us, length us, event | category | flops | bytes accessed | tf_op | source)
XLA Modules:
  0.0 70.3 jit_solution(12166039197626776004)
XLA Ops:
  0.0 0.0 copy-start
  0.0 0.7 copy-done
  0.7 69.0 %gram.1 = f32[1,3,16,512]{3,2,1,0:T(8,128)S(1)} custom-call(f32[4,4,2,2,8,1024]{5,4,3,2,1,0:T(8,128)} %bitcast.2, s32[100,512]{1,0:T(8,128)} %bitcast.3, s32[2,512]{1,0:T(2,128)S(1)} %copy-done), custom_call_target="tpu_custom_call" | custom-call | tf_op jit(solution)/shard_map/gram/pallas_call | solution.py:535
  69.7 0.6 copy.5
Async XLA Ops:
  0.0 0.7 copy-start
where the time goes:
time: 70.5 us; the launch traced here: 70.3 us
  Pallas kernels  69 us (98%)
  local copies, waits for them, and re-layouts  1.33 us (2%)
    pallas_call x1, Pallas kernels, gram(): pl.pallas_call(kernel, out_shape=jax.ShapeDtypeStruct((1, 3, 16, SG), F32...  69 us

commit v1 on v0

--- a/solution.py
+++ b/solution.py
@@ -470,7 +470,7 @@
         tile_d = jnp.concatenate([r4_d[0], r4_d[1]], axis=0)
         out_ref[0, 0] = ordered(tile_d, 0)
         return tile_d
-    for turn, name in enumerate((c1, c3, "d", c0, c2, c3, c1, "d", "tile", c2, c3, c0, c1, c2, c3, c1, c2, c3, c0, c1, c2, c3)):
+    for turn, name in enumerate((c1, c3, "d", c0, c2, c3, c1, "d", c2, c3, c1, c2, c3, "tile", c0, c1, c2, c3, c0, c1, c2, c3)):
         with scope(f"tail{turn}_{name}"):
             if name == "tile":
                 tile_d = finish_d()

time: 70.5 us -> 70 us (level)
  no operation moved by 1% of the time
where the time goes in v1:
time: 70 us; the launch traced here: 69.8 us
  Pallas kernels  68.5 us (98%)
  local copies, waits for them, and re-layouts  1.33 us (2%)
    pallas_call x1, Pallas kernels, gram(): pl.pallas_call(kernel, out_shape=jax.ShapeDtypeStruct((1, 3, 16, SG), F32...  68.5 us

profile of v1, /device:TPU:1, one launch (start us, length us, event | category | flops | bytes accessed | tf_op | source)
XLA Modules:
  0.0 69.8 jit_solution(9410910212796701262)
XLA Ops:
  0.0 0.0 copy-start
  0.0 0.7 copy-done
  0.7 68.5 %gram.1 = f32[1,3,16,512]{3,2,1,0:T(8,128)S(1)} custom-call(f32[4,4,2,2,8,1024]{5,4,3,2,1,0:T(8,128)} %bitcast.2, s32[100,512]{1,0:T(8,128)} %bitcast.3, s32[2,512]{1,0:T(2,128)S(1)} %copy-done), custom_call_target="tpu_custom_call" | custom-call | tf_op jit(solution)/shard_map/gram/pallas_call | solution.py:535
  69.2 0.6 copy.5
Async XLA Ops:
  0.0 0.7 copy-start
